TPU v7x, 128 devices: a whole 4x4x4 slice. The times are simulated.
128 devices in a mesh: pipe: 4 (over y_lo, core), dp: 32 (over y_hi, z, x).
Axes of the slice: x: 4, y: 4 (y_hi: 2, y_lo: 2; y = y_hi * 2 + y_lo), z: 4, core: 2. Of those that a mesh axis runs over, the one named last changes fastest.
Arguments:
- stash: bfloat16 [4, 2, 5120, 6144], P('pipe', None, 'dp'), may hold values from -6 to 6
- attn: bfloat16 [4, 2, 32, 6, 160, 160], P('pipe', None, 'dp'), may hold values from 0 to 0.03930664
- w_value: bfloat16 [4, 6144, 768], P('pipe'), may hold values from -0.078125 to 0.078125
- w_out: bfloat16 [4, 768, 6144], P('pipe'), may hold values from -0.21875 to 0.21875
- out_grad: bfloat16 [2, 5120, 6144], P(None, 'dp', 'pipe'), may hold values from -6 to 6
- order: int32 [2], replicated, may hold values from 0 to 1, each once
- check_rows: int32 [8, 6144], replicated, may hold values from -3 to 3
Outputs:
- grad_value: float32 [4, 6144, 768], P('pipe', 'dp')
- grad_out_t: float32 [4, 6144, 768], P('pipe', 'dp')
- checksums: float32 [4, 2, 8, 768], P('pipe')
- input_grad: bfloat16 [2, 5120, 6144], P(None, 'dp', 'pipe')
Inputs may be any that keep to these rules, and one draw needn't show every extreme that they name: `order`: a permutation of the micro-batches.
All inputs are finite; a program needn't handle non-finite values.
Results may differ from a plain program's by a relative error of at most 0.022.
Values may be sent and summed in bfloat16 or wider, within the bound.
No kernel may reach another device: no remote copies, remote signals or barrier semaphores. Data moves between devices by JAX's collectives and lax.ppermute only.
A program may use at most 192 MiB of HBM per device.

v0:
```python
import jax
import jax.numpy as jnp
from jax import lax
from jax.sharding import PartitionSpec as P


def passed_along(block, axis, distance):
    devices = range(lax.axis_size(axis))
    route = [(i - distance, i) for i in devices if i - distance in devices]
    return lax.ppermute(block, axis, route)


def from_root(array, axis, root):
    mine = lax.axis_index(axis) == root
    return lax.psum(jnp.where(mine, array, jnp.zeros_like(array)), axis)


def on_device(stash, attn, w_value, w_out, out_grad, order, check_rows):
    npipe = lax.axis_size("pipe")
    section = lax.axis_index("pipe")
    inputs = stash[0]
    probs = attn[0][:, 0]
    wv = w_value[0]
    wo = w_out[0]
    micro = inputs.shape[0]
    seq = inputs.shape[1]
    width = inputs.shape[2]
    inner = wv.shape[1]
    heads = probs.shape[1]
    head_dim = inner // heads
    grad_scale = jnp.float32((micro * seq * lax.axis_size("dp")) ** (-0.5))
    check_scale = jnp.float32(width ** (-0.5))
    causal = (jnp.arange(seq)[:, None] >= jnp.arange(seq)[None, :]).astype(jnp.bfloat16)
    top_grad = lax.all_gather(out_grad, "pipe", axis=2, tiled=True)

    def backward_step(operands):
        xm, pm, dy = operands
        weights = pm * causal
        values = jnp.dot(xm, wv, preferred_element_type=jnp.float32).astype(jnp.bfloat16)
        context = jnp.einsum(
            "hij,jhd->ihd",
            weights,
            values.reshape(seq, heads, head_dim),
            preferred_element_type=jnp.float32,
        )
        context = context.reshape(seq, inner).astype(jnp.bfloat16)
        dctx = jnp.dot(dy, wo.T, preferred_element_type=jnp.float32).astype(jnp.bfloat16)
        dvals = jnp.einsum(
            "hij,ihd->jhd",
            weights,
            dctx.reshape(seq, heads, head_dim),
            preferred_element_type=jnp.float32,
        )
        dvals = dvals.reshape(seq, inner).astype(jnp.bfloat16)
        dx = (
            dy.astype(jnp.float32) + jnp.dot(dvals, wv.T, preferred_element_type=jnp.float32)
        ).astype(jnp.bfloat16)
        return (context, dvals, dx)

    def skip_step(operands):
        return (
            jnp.zeros((seq, inner), jnp.bfloat16),
            jnp.zeros((seq, inner), jnp.bfloat16),
            jnp.zeros((seq, width), jnp.bfloat16),
        )

    ctx_store = jnp.zeros((micro, seq, inner), jnp.bfloat16)
    dv_store = jnp.zeros((micro, seq, inner), jnp.bfloat16)
    dy_store = jnp.zeros((micro, seq, width), jnp.bfloat16)
    dx_store = jnp.zeros((micro, seq, width), jnp.bfloat16)
    incoming = jnp.zeros((seq, width), jnp.bfloat16)
    last_turn = micro + npipe - 2
    for turn in range(micro + npipe - 1):
        step = turn - (npipe - 1 - section)
        valid = jnp.logical_and(step >= 0, step < micro)
        slot = jnp.clip(step, 0, micro - 1)
        batch = order[slot]
        dy = jnp.where(
            section == npipe - 1, lax.dynamic_index_in_dim(top_grad, slot, 0, False), incoming
        )
        xm = lax.dynamic_index_in_dim(inputs, batch, 0, False)
        pm = lax.dynamic_index_in_dim(probs, batch, 0, False)
        context, dvals, dx = lax.cond(valid, backward_step, skip_step, (xm, pm, dy))
        ctx_store = jnp.where(
            valid, lax.dynamic_update_index_in_dim(ctx_store, context, batch, 0), ctx_store
        )
        dv_store = jnp.where(
            valid, lax.dynamic_update_index_in_dim(dv_store, dvals, batch, 0), dv_store
        )
        dy_store = jnp.where(
            valid, lax.dynamic_update_index_in_dim(dy_store, dy, batch, 0), dy_store
        )
        dx_store = jnp.where(
            valid, lax.dynamic_update_index_in_dim(dx_store, dx, slot, 0), dx_store
        )
        if turn < last_turn:
            incoming = passed_along(dx, "pipe", -1)
    x_flat = inputs.reshape(micro * seq, width)
    dv_flat = dv_store.reshape(micro * seq, inner)
    dy_flat = dy_store.reshape(micro * seq, width)
    ctx_flat = ctx_store.reshape(micro * seq, inner)
    contract = (((0,), (0,)), ((), ()))
    ck_float = check_rows.astype(jnp.float32)
    rows = width // lax.axis_size("dp")
    columns = x_flat
    grad_v = lax.psum_scatter(
        (
            lax.dot_general(columns, dv_flat, contract, preferred_element_type=jnp.float32)
            * grad_scale
        ).astype(jnp.bfloat16),
        "dp",
        scatter_dimension=0,
        tiled=True,
    ).astype(jnp.float32)
    columns = dy_flat
    grad_o = lax.psum_scatter(
        (
            lax.dot_general(columns, ctx_flat, contract, preferred_element_type=jnp.float32)
            * grad_scale
        ).astype(jnp.bfloat16),
        "dp",
        scatter_dimension=0,
        tiled=True,
    ).astype(jnp.float32)
    first_row = lax.axis_index("dp") * rows
    ck_part = lax.dynamic_slice_in_dim(ck_float, first_row, rows, 1)
    local_checks = check_scale * jnp.stack(
        [
            jnp.dot(ck_part, grad_v, precision=lax.Precision.HIGHEST),
            jnp.dot(ck_part, grad_o, precision=lax.Precision.HIGHEST),
        ]
    )
    check_sum = lax.psum(local_checks, "dp")
    first_grads = from_root(dx_store, "pipe", 0)
    share = width // npipe
    own_part = lax.dynamic_slice_in_dim(first_grads, section * share, share, 2)
    return (grad_v[None], grad_o[None], check_sum[None], own_part)


def solution(mesh):
    return jax.shard_map(
        on_device,
        mesh=mesh,
        in_specs=(
            P("pipe", None, "dp", None),
            P("pipe", None, "dp", None, None, None),
            P("pipe", None, None),
            P("pipe", None, None),
            P(None, "dp", "pipe"),
            P(),
            P(),
        ),
        out_specs=(
            P("pipe", "dp", None),
            P("pipe", "dp", None),
            P("pipe", None, None, None),
            P(None, "dp", "pipe"),
        ),
        check_vma=False,
    )
```

profile of v0, /device:TPU:16, one launch (start us, length us, event | category | flops | bytes accessed | tf_op | source)
XLA Modules:
  0.0 1039.1 jit_solution(13033466347937102646)
XLA Ops:
  8.0 1.5 fusion.131
  11.5 44.0 %all-gather.2.cloned.1.call-done = bf16[2,160,6144]{2,1,0:T(8,128)(2,1)} async-done(((bf16[2,160,1536]{2,1,0:T(8,128)(2,1)}), bf16[2,160,6144]{2,1,0:T(8,128)(2,1)}) %all-gather.2.cloned.1.call-update) | async-done | bytes 3932176 | tf_op jit(solution)/shard_map/all_gather | solution.py:34
  55.5 2.5 broadcast.104.clone
  57.9 4.3 select_dynamic-update-slice_fusion.5
  62.5 1.8 conditional.5
  62.5 1.6 broadcast.92
  67.5 3.3 collective-permute-done
  70.8 5.2 fusion.125
  76.1 3.2 conditional.6
  76.1 1.5 broadcast.94
  77.6 1.5 broadcast_in_dim.112
  86.4 19.1 %collective-permute-done.1 = bf16[160,6144]{1,0:T(8,128)(2,1)S(1)} collective-permute-done((bf16[160,6144]{1,0:T(8,128)(2,1)}, bf16[160,6144]{1,0:T(8,128)(2,1)S(1)}, u32[]{:S(2)}, u32[]{:S(2)}) %collective-permute-start.1) | collective-permute-done | bytes 1966112 | tf_op jit(solution)/shard_map/ppermute | solution.py:10
  106.8 5.4 fusion.124
  112.9 4.6 conditional.7
  112.9 1.5 broadcast.95
  114.5 1.5 broadcast_in_dim.115
  117.6 1.4 collective-permute-start.2
  119.0 2.4 broadcast.104
  121.4 1.7 select_dynamic-update-slice_fusion.4
  123.1 3.9 select_dynamic-update-slice_fusion.3
  127.0 53.4 %collective-permute-done.2 = bf16[160,6144]{1,0:T(8,128)(2,1)S(1)} collective-permute-done((bf16[160,6144]{1,0:T(8,128)(2,1)}, bf16[160,6144]{1,0:T(8,128)(2,1)S(1)}, u32[]{:S(2)}, u32[]{:S(2)}) %collective-permute-start.2) | collective-permute-done | bytes 1966112 | tf_op jit(solution)/shard_map/ppermute | solution.py:10
  180.4 4.1 fusion.123
  184.6 21.8 %conditional.8 = (bf16[160,6144]{1,0:T(8,128)(2,1)}, bf16[1,160,768]{2,1,0:T(8,128)(2,1)}, bf16[1,160,768]{2,1,0:T(8,128)(2,1)S(1)}, bf16[1,160,6144]{2,1,0:T(8,128)(2,1)}) conditional(s32[]{:T(128)} %convert_element_type.329, () %tuple.104, (bf16[160,6144]{1,0:T(8,128)(2,1)S(1)}, bf16[768,6144]{1,0:T(8,128)(2,1)S(1)}, ...), branch_computations={%region_6.7_spmd, %region_7.8_spmd} | conditional | flops 4612700160 | bytes 89258160 | solution.py:83
  185.0 3.9 fusion.81
  189.7 1.5 convolution_convert_fusion.9
  191.3 8.3 fusion.73
  199.6 3.2 copy.226
  202.8 1.8 fusion.82
  207.7 3.5 select_dynamic-update-slice_fusion.2
  211.2 4.2 select_dynamic-update-slice_fusion.1
  215.4 17.1 %collective-permute-done.3 = bf16[160,6144]{1,0:T(8,128)(2,1)S(1)} collective-permute-done((bf16[160,6144]{1,0:T(8,128)(2,1)}, bf16[160,6144]{1,0:T(8,128)(2,1)S(1)}, u32[]{:S(2)}, u32[]{:S(2)}) %collective-permute-start.3) | collective-permute-done | bytes 1966112 | tf_op jit(solution)/shard_map/ppermute | solution.py:10
  232.6 4.0 fusion.122
  236.6 18.0 %conditional.9 = (bf16[1,160,768]{2,1,0:T(8,128)(2,1)}, bf16[1,160,768]{2,1,0:T(8,128)(2,1)}, bf16[1,160,6144]{2,1,0:T(8,128)(2,1)}) conditional(s32[]{:T(128)} %convert_element_type.330, () %tuple.106, (bf16[1,2,160,6144]{3,2,1,0:T(8,128)(2,1)}, s32[]{:T(128)}, bf16[6144,768]{1,0:T(8,128)(2,1)}, bf16[1,2,1,6,160,160]{5,4,3,2,1,0:T(8,128)(2,1)S(1)}, ...), branch_computations={%region_8.9_spmd, %region_9.10_spmd} | conditional | flops 4612700160 | bytes 98173048 | solution.py:83
  236.8 1.4 copy.102
  238.2 7.1 fusion.105
  245.6 4.6 fusion.97
  250.2 1.8 fusion.106
  254.6 4.1 select_dynamic-update-slice_fusion
  258.7 4.2 broadcast_select_fusion
  266.4 9.6 fusion.120
  278.1 9.6 fusion.121
  287.7 12.7 %copy.109 = bf16[6144,768]{1,0:T(8,128)(2,1)} copy(bf16[6144,768]{0,1:T(8,128)(2,1)} %fusion.121) | data formatting | bytes 18874368
  300.4 53.4 %all-reduce.2.cloned.1.call-done = bf16[2,160,6144]{2,1,0:T(8,128)(2,1)} async-done(((bf16[2,160,6144]{2,1,0:T(8,128)(2,1)}), bf16[2,160,6144]{2,1,0:T(8,128)(2,1)}) %all-reduce.2.cloned.1.call-update) | async-done | bytes 3932176 | tf_op jit(solution)/shard_map/psum | solution.py:15
  353.9 2.2 constant_dynamic-slice_fusion
  356.1 245.0 %reduce-scatter.5.cloned.1.call-done = bf16[192,768]{1,0:T(8,128)(2,1)} async-done(((bf16[6144,768]{1,0:T(8,128)(2,1)}), bf16[192,768]{1,0:T(8,128)(2,1)}) %reduce-scatter.5.cloned.1.call-update) | async-done | bytes 294928 | tf_op jit(solution)/shard_map/reduce_scatter | solution.py:116
  601.0 1.3 convolution_bitcast_fusion
  602.3 243.8 %reduce-scatter.7.cloned.1.call-done = bf16[192,768]{1,0:T(8,128)(2,1)} async-done(((bf16[6144,768]{1,0:T(8,128)(2,1)}), bf16[192,768]{1,0:T(8,128)(2,1)}) %reduce-scatter.7.cloned.1.call-update) | async-done | bytes 294928
  847.4 181.8 %psum.14 = f32[1,2,8,768]{3,2,1,0:T(8,128)} all-reduce(f32[1,2,8,768]{3,2,1,0:T(8,128)S(1)} %fusion.127), channel_id=1, replica_groups=mesh['pipe'=4,'dp'=32] {'dp'}, use_global_device_ids=true, to_apply=%region_12.13 | all-reduce | flops 12288 | bytes 98304 | tf_op jit(solution)/shard_map/psum | solution.py:133
  (107 shorter events, 24.1 us)
Async XLA Ops:
  7.2 48.3 %all-gather.2.cloned.1.call-start = ((), (), s32[]{:S(2)}) async-start(), calls=%async_computation.2 | async-start | bytes 4915200 | tf_op jit(solution)/shard_map/all_gather | solution.py:34
  7.9 346.0 %all-reduce.2.cloned.1.call-start = ((), (), s32[]{:S(2)}) async-start(), calls=%async_computation.4 | async-start | bytes 7864320 | tf_op jit(solution)/shard_map/psum | solution.py:15
  55.5 7.0 copy-start.1
  57.9 4.6 copy-start.5
  64.3 6.5 copy-start.6
  64.3 11.7 %copy-start.20 = (bf16[1,160,768]{2,1,0:T(8,128)(2,1)}, bf16[1,160,768]{2,1,0:T(8,128)(2,1)S(1)}, u32[]{:S(2)}) copy-start(bf16[1,160,768]{2,1,0:T(8,128)(2,1)S(1)} %get-tuple-element.362) | copy-start | bytes 737284
  64.4 11.7 %copy-start.22 = (bf16[1,160,768]{2,1,0:T(8,128)(2,1)}, bf16[1,160,768]{2,1,0:T(8,128)(2,1)S(1)}, u32[]{:S(2)}) copy-start(bf16[1,160,768]{2,1,0:T(8,128)(2,1)S(1)} %get-tuple-element.353) | copy-start | bytes 737284
  64.4 6.5 collective-permute-start
  79.3 33.6 %copy-start.17 = (bf16[1,160,768]{2,1,0:T(8,128)(2,1)}, bf16[1,160,768]{2,1,0:T(8,128)(2,1)S(1)}, u32[]{:S(2)}) copy-start(bf16[1,160,768]{2,1,0:T(8,128)(2,1)S(1)} %get-tuple-element.355) | copy-start | bytes 737284
  79.3 26.1 %collective-permute-start.1 = (bf16[160,6144]{1,0:T(8,128)(2,1)}, bf16[160,6144]{1,0:T(8,128)(2,1)S(1)}, u32[]{:S(2)}, u32[]{:S(2)}) collective-permute-start(bf16[160,6144]{1,0:T(8,128)(2,1)} %get-tuple-element.356), channel_id=1, source_target_pairs={{32,0},{64,32},{96,64},{33,1},{65,33},{97,65},{34,2},{66,34},{98,6... | collective-permute-start | bytes 5898248 | tf_op jit(solution)/shard_map/ppermute | solution.py:10
  105.5 1.3 copy-start.14
  106.8 6.1 copy-start.2
  117.6 3.8 copy-start.7
  117.6 62.9 %collective-permute-start.2 = (bf16[160,6144]{1,0:T(8,128)(2,1)}, bf16[160,6144]{1,0:T(8,128)(2,1)S(1)}, u32[]{:S(2)}, u32[]{:S(2)}) collective-permute-start(bf16[160,6144]{1,0:T(8,128)(2,1)} %get-tuple-element.358), channel_id=1, source_target_pairs={{32,0},{64,32},{96,64},{33,1},{65,33},{97,65},{34,2},{66,34},{98,6... | collective-permute-start | bytes 5898248 | tf_op jit(solution)/shard_map/ppermute | solution.py:10
  121.4 63.2 %slice-start.12 = ((s8[9437184]{0:T(1024)(128)(4,1)}), s8[4194304]{0:T(1024)(128)(4,1)S(1)}, s32[]{:S(2)}) async-start(s8[9437184]{0:T(1024)(128)(4,1)} %bitcast.268), calls=%async_computation.18 | async-start | bytes 8388608
  123.1 57.3 %copy-start.3 = (bf16[2,160,6144]{2,1,0:T(8,128)(2,1)S(1)}, bf16[2,160,6144]{2,1,0:T(8,128)(2,1)}, u32[]{:S(2)}) copy-start(bf16[2,160,6144]{2,1,0:T(8,128)(2,1)} %all-gather.2.cloned.1.call-done) | copy-start | bytes 11796484
  123.1 61.5 %slice-start.13 = ((s8[9437184]{0:T(1024)(128)(4,1)}), s8[4194304]{0:T(1024)(128)(4,1)S(1)}, s32[]{:S(2)}) async-start(s8[9437184]{0:T(1024)(128)(4,1)} %bitcast.268), calls=%async_computation.19 | async-start | bytes 8388608
  180.4 4.1 slice-start.14
  189.7 13.1 %slice-start.9 = ((s8[9437184]{0:T(1024)(128)(4,1)}), s8[4194304]{0:T(1024)(128)(4,1)S(1)}, s32[]{:S(2)}) async-start(s8[9437184]{0:T(1024)(128)(4,1)} %bitcast.262), calls=%async_computation.15 | async-start | bytes 8388608 | tf_op jit(solution)/shard_map/cond
  191.2 11.5 %slice-start.10 = ((s8[9437184]{0:T(1024)(128)(4,1)}), s8[4194304]{0:T(1024)(128)(4,1)S(1)}, s32[]{:S(2)}) async-start(s8[9437184]{0:T(1024)(128)(4,1)} %bitcast.262), calls=%async_computation.16 | async-start | bytes 8388608 | tf_op jit(solution)/shard_map/cond
  191.3 11.5 %slice-start.11 = ((s8[9437184]{0:T(1024)(128)(4,1)}), s8[1048576]{0:T(1024)(128)(4,1)S(1)}, s32[]{:S(2)}) async-start(s8[9437184]{0:T(1024)(128)(4,1)} %bitcast.262), calls=%async_computation.17 | async-start | bytes 2097152 | tf_op jit(solution)/shard_map/cond
  199.6 3.2 copy-start.11
  202.8 1.8 copy-start.28
  206.4 9.0 copy-start.24
  206.4 26.1 %collective-permute-start.3 = (bf16[160,6144]{1,0:T(8,128)(2,1)}, bf16[160,6144]{1,0:T(8,128)(2,1)S(1)}, u32[]{:S(2)}, u32[]{:S(2)}) collective-permute-start(bf16[160,6144]{1,0:T(8,128)(2,1)} %get-tuple-element.360), channel_id=1, source_target_pairs={{32,0},{64,32},{96,64},{33,1},{65,33},{97,65},{34,2},{66,34},{98,6... | collective-permute-start | bytes 5898248 | tf_op jit(solution)/shard_map/ppermute | solution.py:10
  211.2 21.4 %copy-start.4 = (bf16[2,160,6144]{2,1,0:T(8,128)(2,1)S(1)}, bf16[2,160,6144]{2,1,0:T(8,128)(2,1)}, u32[]{:S(2)}) copy-start(bf16[2,160,6144]{2,1,0:T(8,128)(2,1)} %all-gather.2.cloned.1.call-done) | copy-start | bytes 11796484
  238.2 7.1 copy-start.13
  238.2 7.4 copy-start
  245.6 4.6 copy-start.12
  262.9 0.9 copy-start.23
  262.9 1.1 copy-start.21
  262.9 1.2 copy-start.18
  263.0 338.1 %reduce-scatter.5.cloned.1.call-start = ((), (), s32[]{:S(2)}) async-start(), calls=%async_computation.3 | async-start | bytes 9732096 | tf_op jit(solution)/shard_map/reduce_scatter | solution.py:116
  276.0 1.0 copy-start.25
  276.1 570.1 %reduce-scatter.7.cloned.1.call-start = ((), (), s32[]{:S(2)}) async-start(), calls=%async_computation.5 | async-start | bytes 9732096
  601.0 430.5 %copy-start.16 = (bf16[192,768]{1,0:T(8,128)(2,1)S(1)}, bf16[192,768]{1,0:T(8,128)(2,1)}, u32[]{:S(2)}) copy-start(bf16[192,768]{1,0:T(8,128)(2,1)} %reduce-scatter.5.cloned.1.call-done) | copy-start | bytes 884740
Sparse Core Ops, SparseCore 0:
  9.7 45.7 all-gather.1
  263.1 90.7 all-reduce.1
  359.2 241.7 reduce-scatter.4
  606.2 239.8 reduce-scatter.6
where the time goes:
time: 1050 us; the launch traced here: 1040 us
  waiting for transfers between devices  680 us (65%)
  blocking collectives  182 us (17%)
  matrix products  51.8 us (5%)
  other arithmetic  49.2 us (5%)
  local copies, waits for them, and re-layouts  45.9 us (4%)
  between operations  23.8 us (2%)
    reduce_scatter x1, waiting for transfers between devices, on_device(): lax.psum_scatter((lax.dot_general(columns, ctx_flat, contract, preferred_...  245 us
    unnamed x5, waiting for transfers between devices  245 us
    psum x1, blocking collectives, on_device(): check_sum = lax.psum(local_checks, 'dp')  182 us
    ppermute x4, waiting for transfers between devices, passed_along(): return lax.ppermute(block, axis, route)  93 us
    psum x1, waiting for transfers between devices, from_root(): return lax.psum(jnp.where(mine, array, jnp.zeros_like(array)), axis)  53.4 us
    all_gather x1, waiting for transfers between devices, on_device(): top_grad = lax.all_gather(out_grad, 'pipe', axis=2, tiled=True)  44 us
    select_n x5, other arithmetic, on_device(): jnp.where(valid, lax.dynamic_update_index_in_dim(dy_store, dy, batch, 0),...  23 us
  transfers between devices with their start and end apart: 8, of which 8 were waited for; matrix products, arithmetic and copies ran while one was open for 5% of the time, Pallas kernels for 0%

commit v1 on v0

--- a/solution.py
+++ b/solution.py
@@ -2,6 +2,13 @@
 import jax.numpy as jnp
 from jax import lax
 from jax.sharding import PartitionSpec as P
+
+
+def swapped_in(x, mesh_axis, dim):
+    n_dev = lax.axis_size(mesh_axis)
+    blocks = jnp.stack([x for _ in range(n_dev)])
+    blocks = lax.all_to_all(blocks, mesh_axis, split_axis=0, concat_axis=0)
+    return jnp.concatenate(blocks, axis=dim)
 
 
 def passed_along(block, axis, distance):
@@ -31,7 +38,7 @@
     grad_scale = jnp.float32((micro * seq * lax.axis_size("dp")) ** (-0.5))
     check_scale = jnp.float32(width ** (-0.5))
     causal = (jnp.arange(seq)[:, None] >= jnp.arange(seq)[None, :]).astype(jnp.bfloat16)
-    top_grad = lax.all_gather(out_grad, "pipe", axis=2, tiled=True)
+    top_grad = swapped_in(out_grad, "pipe", 2)
 
     def backward_step(operands):
         xm, pm, dy = operands

time: 1050 us -> 1000 us (0.952)
  waiting for transfers between devices: 680 us -> 626 us
  local copies, waits for them, and re-layouts: 45.9 us -> 60 us
    reduce_scatter x1, waiting for transfers between devices: 245 us -> 186 us  [on_device(): lax.psum_scatter((lax.dot_general(columns, ctx_flat, contract, preferred_...]
    all_gather x1 -> x0, waiting for transfers between devices: 44 us -> none  [on_device(): top_grad = lax.all_gather(out_grad, 'pipe', axis=2, tiled=True)]
    all_to_all x0 -> x1, waiting for transfers between devices: none -> 42.7 us  [swapped_in(): blocks = lax.all_to_all(blocks, mesh_axis, split_axis=0, concat_axis=0)]
    unnamed x43 -> x61, local copies, waits for them, and re-layouts: 18.5 us -> 28 us
    unnamed x5 -> x4, waiting for transfers between devices: 245 us -> 244 us
where the time goes in v1:
time: 1000 us; the launch traced here: 995 us
  waiting for transfers between devices  626 us (63%)
  blocking collectives  182 us (18%)
  local copies, waits for them, and re-layouts  60 us (6%)
  matrix products  50.2 us (5%)
  other arithmetic  40.1 us (4%)
  between operations  26 us (3%)
  starting transfers between devices  10.5 us (1%)
    unnamed x4, waiting for transfers between devices  244 us
    reduce_scatter x1, waiting for transfers between devices, on_device(): lax.psum_scatter((lax.dot_general(columns, ctx_flat, contract, preferred_...  186 us
    psum x1, blocking collectives, on_device(): check_sum = lax.psum(local_checks, 'dp')  182 us
    ppermute x4, waiting for transfers between devices, passed_along(): return lax.ppermute(block, axis, route)  91.2 us
    psum x1, waiting for transfers between devices, from_root(): return lax.psum(jnp.where(mine, array, jnp.zeros_like(array)), axis)  62 us
    all_to_all x1, waiting for transfers between devices, swapped_in(): blocks = lax.all_to_all(blocks, mesh_axis, split_axis=0, concat_axis=0)  42.7 us
    unnamed x61, local copies, waits for them, and re-layouts  28 us
  transfers between devices with their start and end apart: 8, of which 8 were waited for; matrix products, arithmetic and copies ran while one was open for 5% of the time, Pallas kernels for 0%

profile of v1, /device:TPU:16, one launch (start us, length us, event | category | flops | bytes accessed | tf_op | source)
XLA Modules:
  0.0 995.1 jit_solution(7627025668109115449)
XLA Ops:
  8.0 3.5 stack.16
  11.5 4.9 all-to-all-start
  19.1 42.7 %all-to-all-done = bf16[4,2,160,1536]{3,2,1,0:T(8,128)(2,1)} async-done(((bf16[4,2,160,1536]{3,2,1,0:T(8,128)(2,1)}), bf16[4,2,160,1536]{3,2,1,0:T(8,128)(2,1)}, u32[]{:S(2)}, u32[]{:S(2)}) %all-to-all-start) | async-done | bytes 3932192 | tf_op jit(solution)/shard_map/all_to_all | solution.py:10
  61.8 2.8 copy.163
  66.9 2.9 slice-done.14
  69.9 3.0 conditional.5
  69.9 1.5 broadcast.94
  71.4 1.5 broadcast_in_dim.109
  77.5 2.9 collective-permute-done
  81.6 5.3 fusion.125
  86.9 3.2 conditional.6
  86.9 1.5 broadcast.96
  88.4 1.5 broadcast_in_dim.112
  97.3 18.2 %collective-permute-done.1 = bf16[160,6144]{1,0:T(8,128)(2,1)S(1)} collective-permute-done((bf16[160,6144]{1,0:T(8,128)(2,1)}, bf16[160,6144]{1,0:T(8,128)(2,1)S(1)}, u32[]{:S(2)}, u32[]{:S(2)}) %collective-permute-start.1) | collective-permute-done | bytes 1966112 | tf_op jit(solution)/shard_map/ppermute | solution.py:17
  116.7 5.4 fusion.124
  122.8 4.8 conditional.7
  122.8 1.5 broadcast.97
  124.3 1.5 broadcast_in_dim.115
  129.0 2.5 broadcast.106
  131.4 1.6 select_dynamic-update-slice_fusion.4
  133.1 4.1 select_dynamic-update-slice_fusion.3
  137.1 53.1 %collective-permute-done.2 = bf16[160,6144]{1,0:T(8,128)(2,1)S(1)} collective-permute-done((bf16[160,6144]{1,0:T(8,128)(2,1)}, bf16[160,6144]{1,0:T(8,128)(2,1)S(1)}, u32[]{:S(2)}, u32[]{:S(2)}) %collective-permute-start.2) | collective-permute-done | bytes 1966112 | tf_op jit(solution)/shard_map/ppermute | solution.py:17
  191.4 1.9 copy-done.7
  193.3 21.5 %conditional.8 = (bf16[160,6144]{1,0:T(8,128)(2,1)}, bf16[1,160,768]{2,1,0:T(8,128)(2,1)}, bf16[1,160,768]{2,1,0:T(8,128)(2,1)S(1)}, bf16[1,160,6144]{2,1,0:T(8,128)(2,1)}) conditional(s32[]{:T(128)} %convert_element_type.329, () %tuple.104, (bf16[160,6144]{1,0:T(8,128)(2,1)S(1)}, bf16[768,6144]{1,0:T(8,128)(2,1)S(1)}, ...), branch_computations={%region_6.7_spmd, %region_7.8_spmd} | conditional | flops 4612700160 | bytes 89258160 | solution.py:90
  193.5 3.9 fusion.81
  198.2 1.5 convolution_convert_fusion.9
  199.7 8.3 fusion.73
  208.0 3.2 copy.264
  211.2 1.8 fusion.82
  216.2 3.6 select_dynamic-update-slice_fusion.2
  219.8 4.2 select_dynamic-update-slice_fusion.1
  223.9 17.1 %collective-permute-done.3 = bf16[160,6144]{1,0:T(8,128)(2,1)S(1)} collective-permute-done((bf16[160,6144]{1,0:T(8,128)(2,1)}, bf16[160,6144]{1,0:T(8,128)(2,1)S(1)}, u32[]{:S(2)}, u32[]{:S(2)}) %collective-permute-start.3) | collective-permute-done | bytes 1966112 | tf_op jit(solution)/shard_map/ppermute | solution.py:17
  242.3 1.9 copy-done.9
  244.2 18.1 %conditional.9 = (bf16[1,160,768]{2,1,0:T(8,128)(2,1)}, bf16[1,160,768]{2,1,0:T(8,128)(2,1)}, bf16[1,160,6144]{2,1,0:T(8,128)(2,1)}) conditional(s32[]{:T(128)} %convert_element_type.330, () %tuple.106, (bf16[1,2,160,6144]{3,2,1,0:T(8,128)(2,1)}, s32[]{:T(128)}, bf16[6144,768]{1,0:T(8,128)(2,1)}, bf16[1,2,1,6,160,160]{5,4,3,2,1,0:T(8,128)(2,1)S(1)}, ...), branch_computations={%region_8.9_spmd, %region_9.10_spmd} | conditional | flops 4612700160 | bytes 98173048 | solution.py:90
  244.4 1.4 copy.139
  245.8 7.1 fusion.105
  253.2 4.6 fusion.97
  257.9 1.8 fusion.106
  262.3 4.1 select_dynamic-update-slice_fusion
  266.4 4.2 broadcast_select_fusion
  274.2 7.6 fusion.120
  283.8 10.0 %fusion.121 = bf16[6144,768]{0,1:T(8,128)(2,1)} fusion(bf16[320,768]{1,0:T(8,128)(2,1)S(1)} %bitcast.281, bf16[320,6144]{1,0:T(8,128)(2,1)} %bitcast.282), kind=kOutput, calls=%fused_computation.128 | convolution fusion | flops 3029336064 | bytes 13860864 | tf_op jit(solution)/shard_map/dot_general | solution.py:115
  293.8 12.1 %copy.146 = bf16[6144,768]{1,0:T(8,128)(2,1)} copy(bf16[6144,768]{0,1:T(8,128)(2,1)} %fusion.121) | data formatting | bytes 18874368
  306.0 62.0 %all-reduce.2.cloned.1.call-done = bf16[2,160,6144]{2,1,0:T(8,128)(2,1)} async-done(((bf16[2,160,6144]{2,1,0:T(8,128)(2,1)}), bf16[2,160,6144]{2,1,0:T(8,128)(2,1)}) %all-reduce.2.cloned.1.call-update) | async-done | bytes 3932176 | tf_op jit(solution)/shard_map/psum | solution.py:22
  367.9 2.3 constant_dynamic-slice_fusion
  370.2 185.7 %reduce-scatter.5.cloned.1.call-done = bf16[192,768]{1,0:T(8,128)(2,1)} async-done(((bf16[6144,768]{1,0:T(8,128)(2,1)}), bf16[192,768]{1,0:T(8,128)(2,1)}) %reduce-scatter.5.cloned.1.call-update) | async-done | bytes 294928 | tf_op jit(solution)/shard_map/reduce_scatter | solution.py:123
  557.1 244.2 %reduce-scatter.7.cloned.1.call-done = bf16[192,768]{1,0:T(8,128)(2,1)} async-done(((bf16[6144,768]{1,0:T(8,128)(2,1)}), bf16[192,768]{1,0:T(8,128)(2,1)}) %reduce-scatter.7.cloned.1.call-update) | async-done | bytes 294928
  802.6 181.5 %psum.14 = f32[1,2,8,768]{3,2,1,0:T(8,128)} all-reduce(f32[1,2,8,768]{3,2,1,0:T(8,128)S(1)} %fusion.127), channel_id=1, replica_groups=mesh['pipe'=4,'dp'=32] {'dp'}, use_global_device_ids=true, to_apply=%region_12.13 | all-reduce | flops 12288 | bytes 98304 | tf_op jit(solution)/shard_map/psum | solution.py:140
  (127 shorter events, 33.6 us)
Async XLA Ops:
  11.5 5.0 copy-start.34
  11.5 55.4 %slice-start.12 = ((s8[9437184]{0:T(1024)(128)(4,1)}), s8[1048576]{0:T(1024)(128)(4,1)S(1)}, s32[]{:S(2)}) async-start(s8[9437184]{0:T(1024)(128)(4,1)} %bitcast.269), calls=%async_computation.18 | async-start | bytes 2097152
  11.5 50.3 %all-to-all-start = ((bf16[4,2,160,1536]{3,2,1,0:T(8,128)(2,1)}), bf16[4,2,160,1536]{3,2,1,0:T(8,128)(2,1)}, u32[]{:S(2)}, u32[]{:S(2)}) async-start(bf16[4,2,160,1536]{3,2,1,0:T(8,128)(2,1)} %stack.16), calls=%async_computation | async-start | bytes 7864320 | tf_op jit(solution)/shard_map/all_to_all | solution.py:10
  16.4 351.5 %all-reduce.2.cloned.1.call-start = ((), (), s32[]{:S(2)}) async-start(), calls=%async_computation.4 | async-start | bytes 7864320 | tf_op jit(solution)/shard_map/psum | solution.py:22
  61.8 5.1 slice-start.13
  64.6 2.0 copy-start.2
  64.6 5.2 slice-start.14
  65.1 4.8 copy-start.11
  66.6 3.3 copy-start.5
  72.9 0.7 copy-start.25
  73.6 0.7 copy-start.27
  74.3 6.1 collective-permute-start
  80.4 1.3 copy-start.19
  90.1 32.7 %copy-start.22 = (bf16[1,160,768]{2,1,0:T(8,128)(2,1)}, bf16[1,160,768]{2,1,0:T(8,128)(2,1)S(1)}, u32[]{:S(2)}) copy-start(bf16[1,160,768]{2,1,0:T(8,128)(2,1)S(1)} %get-tuple-element.355) | copy-start | bytes 737284
  90.1 25.3 %collective-permute-start.1 = (bf16[160,6144]{1,0:T(8,128)(2,1)}, bf16[160,6144]{1,0:T(8,128)(2,1)S(1)}, u32[]{:S(2)}, u32[]{:S(2)}) collective-permute-start(bf16[160,6144]{1,0:T(8,128)(2,1)} %get-tuple-element.356), channel_id=1, source_target_pairs={{32,0},{64,32},{96,64},{33,1},{65,33},{97,65},{34,2},{66,34},{98,6... | collective-permute-start | bytes 5898248 | tf_op jit(solution)/shard_map/ppermute | solution.py:17
  115.4 1.3 copy-start.18
  116.7 6.1 copy-start.1
  127.7 62.5 %collective-permute-start.2 = (bf16[160,6144]{1,0:T(8,128)(2,1)}, bf16[160,6144]{1,0:T(8,128)(2,1)S(1)}, u32[]{:S(2)}, u32[]{:S(2)}) collective-permute-start(bf16[160,6144]{1,0:T(8,128)(2,1)} %get-tuple-element.358), channel_id=1, source_target_pairs={{32,0},{64,32},{96,64},{33,1},{65,33},{97,65},{34,2},{66,34},{98,6... | collective-permute-start | bytes 5898248 | tf_op jit(solution)/shard_map/ppermute | solution.py:17
  129.0 61.2 %copy-start.6 = (bf16[2,160,6144]{2,1,0:T(8,128)(2,1)S(1)}, bf16[2,160,6144]{2,1,0:T(8,128)(2,1)}, u32[]{:S(2)}) copy-start(bf16[2,160,6144]{2,1,0:T(8,128)(2,1)} %get-tuple-element.536) | copy-start | bytes 11796484
  131.4 60.0 %slice-start.15 = ((s8[9437184]{0:T(1024)(128)(4,1)}), s8[4194304]{0:T(1024)(128)(4,1)S(1)}, s32[]{:S(2)}) async-start(s8[9437184]{0:T(1024)(128)(4,1)} %bitcast.273), calls=%async_computation.21 | async-start | bytes 8388608
  133.1 57.1 %copy-start.3 = (bf16[4,2,20,8,1536]{4,3,0,2,1:T(8,128)(2,1)S(1)}, bf16[4,2,20,8,1536]{4,3,0,2,1:T(8,128)(2,1)}, u32[]{:S(2)}) copy-start(bf16[4,2,20,8,1536]{4,3,0,2,1:T(8,128)(2,1)} %copy-done.2) | copy-start | bytes 11796484
  133.1 58.4 %slice-start.16 = ((s8[9437184]{0:T(1024)(128)(4,1)}), s8[4194304]{0:T(1024)(128)(4,1)S(1)}, s32[]{:S(2)}) async-start(s8[9437184]{0:T(1024)(128)(4,1)} %bitcast.273), calls=%async_computation.22 | async-start | bytes 8388608
  190.2 1.2 slice-start.17
  191.4 1.9 copy-start.7
  198.2 13.1 %slice-start.9 = ((s8[9437184]{0:T(1024)(128)(4,1)}), s8[4194304]{0:T(1024)(128)(4,1)S(1)}, s32[]{:S(2)}) async-start(s8[9437184]{0:T(1024)(128)(4,1)} %bitcast.265), calls=%async_computation.15 | async-start | bytes 8388608 | tf_op jit(solution)/shard_map/cond
  199.7 11.5 %slice-start.10 = ((s8[9437184]{0:T(1024)(128)(4,1)}), s8[4194304]{0:T(1024)(128)(4,1)S(1)}, s32[]{:S(2)}) async-start(s8[9437184]{0:T(1024)(128)(4,1)} %bitcast.265), calls=%async_computation.16 | async-start | bytes 8388608 | tf_op jit(solution)/shard_map/cond
  199.7 11.5 %slice-start.11 = ((s8[9437184]{0:T(1024)(128)(4,1)}), s8[1048576]{0:T(1024)(128)(4,1)S(1)}, s32[]{:S(2)}) async-start(s8[9437184]{0:T(1024)(128)(4,1)} %bitcast.265), calls=%async_computation.17 | async-start | bytes 2097152 | tf_op jit(solution)/shard_map/cond
  208.0 3.2 copy-start.15
  211.2 1.8 copy-start.33
  214.9 9.1 copy-start.29
  214.9 26.2 %collective-permute-start.3 = (bf16[160,6144]{1,0:T(8,128)(2,1)}, bf16[160,6144]{1,0:T(8,128)(2,1)S(1)}, u32[]{:S(2)}, u32[]{:S(2)}) collective-permute-start(bf16[160,6144]{1,0:T(8,128)(2,1)} %get-tuple-element.360), channel_id=1, source_target_pairs={{32,0},{64,32},{96,64},{33,1},{65,33},{97,65},{34,2},{66,34},{98,6... | collective-permute-start | bytes 5898248 | tf_op jit(solution)/shard_map/ppermute | solution.py:17
  216.2 24.9 %copy-start.8 = (bf16[2,160,6144]{2,1,0:T(8,128)(2,1)S(1)}, bf16[2,160,6144]{2,1,0:T(8,128)(2,1)}, u32[]{:S(2)}) copy-start(bf16[2,160,6144]{2,1,0:T(8,128)(2,1)} %copy-done.7) | copy-start | bytes 11796484
  219.8 21.3 %copy-start.4 = (bf16[4,2,20,8,1536]{4,3,0,2,1:T(8,128)(2,1)S(1)}, bf16[4,2,20,8,1536]{4,3,0,2,1:T(8,128)(2,1)}, u32[]{:S(2)}) copy-start(bf16[4,2,20,8,1536]{4,3,0,2,1:T(8,128)(2,1)} %copy-done.2) | copy-start | bytes 11796484
  242.3 1.9 copy-start.9
  245.8 7.1 copy-start.17
  245.8 7.4 copy-start
  253.2 4.7 copy-start.16
  270.6 0.9 copy-start.28
  270.6 1.1 copy-start.26
  270.6 1.2 copy-start.23
  270.6 285.2 %reduce-scatter.5.cloned.1.call-start = ((), (), s32[]{:S(2)}) async-start(), calls=%async_computation.3 | async-start | bytes 9732096 | tf_op jit(solution)/shard_map/reduce_scatter | solution.py:123
  270.7 3.5 copy-start.10
  281.8 0.9 copy-start.30
  281.8 519.5 %reduce-scatter.7.cloned.1.call-start = ((), (), s32[]{:S(2)}) async-start(), calls=%async_computation.5 | async-start | bytes 9732096
  555.8 430.5 %copy-start.21 = (bf16[192,768]{1,0:T(8,128)(2,1)S(1)}, bf16[192,768]{1,0:T(8,128)(2,1)}, u32[]{:S(2)}) copy-start(bf16[192,768]{1,0:T(8,128)(2,1)} %reduce-scatter.5.cloned.1.call-done) | copy-start | bytes 884740
Sparse Core Ops, SparseCore 0:
  270.7 97.1 all-reduce.1
Sparse Core Ops, SparseCore 1:
  281.9 273.9 reduce-scatter.4
  561.1 240.2 reduce-scatter.6
